TPU v7x, 32 devices: a whole 2x2x4 slice. The times are simulated.
32 devices in a mesh: groups: 2 (over x), grid: 4 (over y, core), head: 4 (over z).
Axes of the slice: x: 2, y: 2, z: 4, core: 2. Of those that a mesh axis runs over, the one named last changes fastest.
Arguments:
- grid_x: bfloat16 [16384, 100], P(('groups', 'grid')), parts along dimension 0, may hold values from -6 to 6
- mesh_h: bfloat16 [2048, 1024], P(('groups', 'grid')), parts along dimension 0, may hold values from -6 to 6
- w_in: bfloat16 [100, 1024], replicated, may hold values from -0.625 to 0.625
- w_q: bfloat16 [1024, 1024], P(None, 'head'), may hold values from -0.1875 to 0.1875
- w_kv: bfloat16 [1024, 2, 1024], P(None, None, 'head'), may hold values from -0.1875 to 0.1875
- w_o: bfloat16 [1024, 1024], P('head'), may hold values from -0.1875 to 0.1875
- w_pqkv: bfloat16 [1024, 3, 1024], P(None, None, 'head'), may hold values from -0.1875 to 0.1875
- w_po: bfloat16 [1024, 1024], P('head'), may hold values from -0.1875 to 0.1875
- edge_src: int32 [4, 4, 256], P('grid'), may hold values from 0 to 2047
- edge_dst: int32 [4, 4, 256], P('grid'), may hold values from 0 to 255
- edge_count: int32 [4, 4], P('grid'), may hold values from 1 to 256, as said below
- win_idx: int32 [1024, 32], P('grid'), may hold values from 0 to 255
- cot: bfloat16 [2048, 1024], P(('groups', 'grid')), parts along dimension 0, may hold values from -6 to 6
Outputs:
- hm_out: bfloat16 [2048, 1024], P(('groups', 'grid'), 'head'), parts along dimension 0
- grad_wkv: float32 [2048, 2, 1024], P(('groups', 'grid'), None, 'head'), parts along dimension 0
There are 2 independent parts, one for each index of `groups`. A program takes and returns all parts, laid end to end along the dimension named above; an argument that names none is the same for every part. Nothing has to cross between parts.
Inputs may be any that keep to these rules, and one draw needn't show every extreme that they name: edge_src[s, r, e] is a row among the 2048 grid rows of grid block s. edge_dst[r, s, e] is a node among the 256 mesh nodes of mesh block r. edge_count[r, s] counts the live slots, from the first, of the edges from grid block s to mesh block r; in every draw one r has 256 live slots from every s. win_idx[i] names nodes of the mesh block of node i by their index in that block; repeats count as often as they appear.
All inputs are finite; a program needn't handle non-finite values.
Results may differ from a plain program's by a relative error of at most 0.029.
Values may be sent and summed in bfloat16 or wider, within the bound.
A program may use at most 64 MiB of HBM per device.

v0:
```python
import math

import jax
import jax.numpy as jnp
from jax import lax
from jax.sharding import PartitionSpec as P

HEAD_SIZE = 64


norm_eps = 1e-05
cap_limit = 30.0
slot_group = 32
highest = lax.Precision.HIGHEST


def layer_norm(values):
    row_mean = jnp.mean(values, axis=-1, keepdims=True)
    centred_input = values - row_mean
    var = jnp.mean(centred_input * centred_input, axis=-1, keepdims=True)
    return centred_input * lax.rsqrt(var + norm_eps)


def embed(rows_x, w_in):
    return layer_norm(jnp.dot(rows_x, w_in, preferred_element_type=jnp.float32)).astype(
        jnp.bfloat16
    )


def bf_round(values):
    return lax.optimization_barrier(values.astype(jnp.bfloat16)).astype(jnp.float32)


def node_sums(onehot, values):
    flat = values.reshape(values.shape[0], -1)
    summed = lax.dot_general(
        onehot,
        flat,
        (((0,), (0,)), ((), ())),
        precision=highest,
        preferred_element_type=jnp.float32,
    )
    return summed.reshape((onehot.shape[1],) + values.shape[1:])


def slot_rows(onehot, values):
    flat = values.reshape(values.shape[0], -1)
    picked = jnp.dot(onehot, flat, precision=highest, preferred_element_type=jnp.float32)
    return picked.reshape((onehot.shape[0],) + values.shape[1:])


def body(
    grid_x, mesh_h, w_in, w_q, w_kv, w_o, w_pqkv, w_po, edge_src, edge_dst, edge_count, win_idx, cot
):
    float_value = jnp.float32
    bfloat_value = jnp.bfloat16
    n_grid = lax.axis_size("grid")
    cols = w_q.shape[1]
    width = mesh_h.shape[1]
    mesh_rows = mesh_h.shape[0]
    heads_dev = cols // HEAD_SIZE
    cap = edge_src.shape[2]
    slots = n_grid * cap
    scale = 1.0 / math.sqrt(HEAD_SIZE)
    contract_last = (((1,), (1,)), ((), ()))
    kv_flat = w_kv.reshape(width, 2 * cols)
    qkv_flat = w_pqkv.reshape(width, 3 * cols)
    send_rows = edge_src[0].reshape(slots)
    dest = edge_dst[0].reshape(slots)
    live = (
        (lax.broadcasted_iota(jnp.int32, (n_grid, cap), 1) < edge_count[0][:, None])
        .astype(float_value)
        .reshape(slots)
    )
    onehot = (dest[:, None] == lax.broadcasted_iota(jnp.int32, (1, mesh_rows), 1)).astype(
        float_value
    )
    channels = grid_x.shape[1]
    outgoing = jnp.take(grid_x, send_rows, axis=0).reshape(
        n_grid, cap // slot_group, slot_group * channels
    )
    received = lax.all_to_all(outgoing, "grid", split_axis=0, concat_axis=0, tiled=True)
    sources = received.shape[0]
    items = received.shape[1]
    rows = received.reshape(sources, items * slot_group, channels)

    def one_source(block):
        normed = embed(block, w_in)
        return (
            normed,
            jnp.dot(normed, kv_flat, preferred_element_type=float_value).astype(bfloat_value),
        )

    normed, kv_rows = lax.map(one_source, rows)
    edge_h = normed.reshape(sources, items, slot_group * width)
    edge_kv = kv_rows.reshape(sources, items, slot_group * 2 * cols)
    edge_rows = edge_h.reshape(slots, width)
    edge_kv = edge_kv.reshape(slots, 2 * cols)
    mesh_normed = layer_norm(mesh_h.astype(float_value)).astype(bfloat_value)
    query = jnp.dot(mesh_normed, w_q, preferred_element_type=float_value).astype(bfloat_value)
    self_kv = jnp.dot(mesh_normed, kv_flat, preferred_element_type=float_value).astype(bfloat_value)
    q_self = query.astype(float_value).reshape(mesh_rows, heads_dev, HEAD_SIZE)
    k_self = self_kv[:, :cols].astype(float_value).reshape(mesh_rows, heads_dev, HEAD_SIZE)
    v_self = self_kv[:, cols:].astype(float_value).reshape(mesh_rows, heads_dev, HEAD_SIZE)
    q_edge = slot_rows(onehot, q_self)
    k_edge = edge_kv[:, :cols].astype(float_value).reshape(slots, heads_dev, HEAD_SIZE)
    v_edge = edge_kv[:, cols:].astype(float_value).reshape(slots, heads_dev, HEAD_SIZE)
    tanh_edge = jnp.tanh(jnp.sum(q_edge * k_edge, axis=2) * scale / cap_limit)
    tanh_self = jnp.tanh(jnp.sum(q_self * k_self, axis=2) * scale / cap_limit)
    weight_edge = jnp.exp(cap_limit * tanh_edge) * live[:, None]
    weight_self = jnp.exp(cap_limit * tanh_self)
    denom = weight_self + node_sums(onehot, weight_edge)
    prob_edge = weight_edge / slot_rows(onehot, denom)
    prob_self = weight_self / denom
    pe_round = bf_round(prob_edge)
    ps_round = bf_round(prob_self)
    mixed = (
        (node_sums(onehot, pe_round[:, :, None] * v_edge) + ps_round[:, :, None] * v_self)
        .reshape(mesh_rows, cols)
        .astype(bfloat_value)
    )
    enc_part = jnp.dot(mixed, w_o, preferred_element_type=float_value)
    hm1 = mesh_h.astype(float_value) + lax.psum(enc_part.astype(jnp.bfloat16), "head").astype(
        jnp.float32
    )
    row_mean = jnp.mean(hm1, axis=1, keepdims=True)
    centred_input = hm1 - row_mean
    inverse_deviation = lax.rsqrt(
        jnp.mean(centred_input * centred_input, axis=1, keepdims=True) + norm_eps
    )
    normalized_input = centred_input * inverse_deviation
    processor_normed = normalized_input.astype(bfloat_value)
    qkv = jnp.dot(processor_normed, qkv_flat, preferred_element_type=float_value).astype(
        bfloat_value
    )
    q2 = qkv[:, :cols].reshape(mesh_rows, heads_dev, HEAD_SIZE)
    k2 = qkv[:, cols : 2 * cols].reshape(mesh_rows, heads_dev, HEAD_SIZE)
    v2 = qkv[:, 2 * cols :].reshape(mesh_rows, heads_dev, HEAD_SIZE)
    members = jnp.sum(
        (win_idx[:, :, None] == lax.broadcasted_iota(jnp.int32, (1, 1, mesh_rows), 2)).astype(
            float_value
        ),
        axis=1,
    )
    tanh2 = jnp.tanh(
        jnp.einsum("ihd,jhd->hij", q2, k2, preferred_element_type=float_value) * scale / cap_limit
    )
    weight2 = members[None] * jnp.exp(cap_limit * tanh2)
    prob2 = weight2 / jnp.sum(weight2, axis=2, keepdims=True)
    p2_round = prob2.astype(bfloat_value)
    attended = (
        jnp.einsum("hij,jhd->ihd", p2_round, v2, preferred_element_type=float_value)
        .reshape(mesh_rows, cols)
        .astype(bfloat_value)
    )
    out_part = jnp.dot(attended, w_po, preferred_element_type=float_value)
    own_cols = lax.dynamic_slice_in_dim(hm1, lax.axis_index("head") * cols, cols, 1)
    hm_out = (
        own_cols
        + lax.psum_scatter(
            out_part.astype(jnp.bfloat16), "head", scatter_dimension=1, tiled=True
        ).astype(jnp.float32)
    ).astype(bfloat_value)
    d_att = (
        lax.dot_general(cot, w_po, contract_last, preferred_element_type=float_value)
        .astype(bfloat_value)
        .reshape(mesh_rows, heads_dev, HEAD_SIZE)
    )
    dprob2 = jnp.einsum("ihd,jhd->hij", d_att, v2, preferred_element_type=float_value)
    dscore2 = prob2 * (dprob2 - jnp.sum(prob2 * dprob2, axis=2, keepdims=True))
    dz2 = (dscore2 * (1.0 - tanh2 * tanh2) * scale).astype(bfloat_value)
    d_q = jnp.einsum("hij,jhd->ihd", dz2, k2, preferred_element_type=float_value).astype(
        bfloat_value
    )
    d_k = jnp.einsum("hij,ihd->jhd", dz2, q2, preferred_element_type=float_value).astype(
        bfloat_value
    )
    d_v = jnp.einsum("hij,ihd->jhd", p2_round, d_att, preferred_element_type=float_value).astype(
        bfloat_value
    )
    d_qkv = jnp.concatenate(
        [d_q.reshape(mesh_rows, cols), d_k.reshape(mesh_rows, cols), d_v.reshape(mesh_rows, cols)],
        axis=1,
    )
    d_part = lax.dot_general(d_qkv, qkv_flat, contract_last, preferred_element_type=float_value)
    normed_gradient = lax.psum(d_part.astype(jnp.bfloat16), "head").astype(jnp.float32)
    hidden_minus_gradient = (
        cot.astype(float_value)
        + inverse_deviation
        * (
            normed_gradient
            - jnp.mean(normed_gradient, axis=1, keepdims=True)
            - normalized_input * jnp.mean(normed_gradient * normalized_input, axis=1, keepdims=True)
        )
    ).astype(bfloat_value)
    d_mixed = lax.dot_general(
        hidden_minus_gradient, w_o, contract_last, preferred_element_type=float_value
    ).astype(bfloat_value)
    dm_self = d_mixed.astype(float_value).reshape(mesh_rows, heads_dev, HEAD_SIZE)
    dm_edge = slot_rows(onehot, dm_self)
    dprob_edge = jnp.sum(dm_edge * v_edge, axis=2)
    dprob_self = jnp.sum(dm_self * v_self, axis=2)
    inner = prob_self * dprob_self + node_sums(onehot, prob_edge * dprob_edge)
    dz_edge = (
        prob_edge * (dprob_edge - slot_rows(onehot, inner)) * (1.0 - tanh_edge * tanh_edge) * scale
    )
    dz_self = prob_self * (dprob_self - inner) * (1.0 - tanh_self * tanh_self) * scale
    edge_grad = jnp.concatenate(
        [
            (dz_edge[:, :, None] * q_edge).reshape(slots, cols),
            (pe_round[:, :, None] * dm_edge).reshape(slots, cols),
        ],
        axis=1,
    ).astype(bfloat_value)
    self_grad = jnp.concatenate(
        [
            (dz_self[:, :, None] * q_self).reshape(mesh_rows, cols),
            (ps_round[:, :, None] * dm_self).reshape(mesh_rows, cols),
        ],
        axis=1,
    ).astype(bfloat_value)
    dims = (((0,), (0,)), ((), ()))
    total = lax.dot_general(edge_rows, edge_grad, dims, preferred_element_type=float_value)
    grad_rows = lax.psum_scatter(
        (
            total
            + lax.dot_general(mesh_normed, self_grad, dims, preferred_element_type=float_value)
        ).astype(jnp.bfloat16),
        "grid",
        scatter_dimension=0,
        tiled=True,
    ).astype(jnp.float32)
    return (hm_out, grad_rows.reshape(width // n_grid, 2, cols))


def solution(mesh):
    placed = (
        P(("groups", "grid"), None),
        P(("groups", "grid"), None),
        P(),
        P(None, "head"),
        P(None, None, "head"),
        P("head", None),
        P(None, None, "head"),
        P("head", None),
        P("grid", None, None),
        P("grid", None, None),
        P("grid", None),
        P("grid", None),
        P(("groups", "grid"), None),
    )
    return jax.shard_map(
        body,
        mesh=mesh,
        in_specs=placed,
        out_specs=(P(("groups", "grid"), "head"), P(("groups", "grid"), None, "head")),
        check_vma=False,
    )
```

profile of v0, /device:TPU:0, one launch (start us, length us, event | category | flops | bytes accessed | tf_op | source)
XLA Modules:
  0.0 202.8 jit_solution(9742783141080785076)
XLA Ops:
  7.2 1.4 copy.41
  10.1 3.2 %gather_fusion = bf16[1024,100]{1,0:T(8,128)(2,1)S(1)} fusion(bf16[2048,100]{1,0:T(8,128)(2,1)S(1)} %copy.41, s32[1024]{0:T(1024)S(1)} %broadcast_clamp_fusion), kind=kCustom, calls=%fused_computation | custom fusion | bytes 413696 | tf_op jit(solution)/shard_map/jit(_take)/gather | solution.py:79
  15.1 4.2 %all-to-all-start = ((bf16[4,8,3200]{2,1,0:T(8,128)(2,1)}), bf16[4,8,3200]{2,1,0:T(8,128)(2,1)S(1)}, u32[]{:S(2)}, u32[]{:S(2)}) async-start(bf16[4,8,3200]{2,1,0:T(8,128)(2,1)} %broadcast_select_fusion), calls=%async_computation | async-start | bytes 409600 | tf_op jit(solution)/shard_map/all_to_all | solution.py:82
  20.8 1.6 bitcast_reduce_fusion.2
  22.4 2.3 %all-to-all-done = bf16[4,8,3200]{2,1,0:T(8,128)(2,1)S(1)} async-done(((bf16[4,8,3200]{2,1,0:T(8,128)(2,1)}), bf16[4,8,3200]{2,1,0:T(8,128)(2,1)S(1)}, u32[]{:S(2)}, u32[]{:S(2)}) %all-to-all-start) | async-done | bytes 204832 | tf_op jit(solution)/shard_map/all_to_all | solution.py:82
  25.7 11.3 %while.12 = (s32[]{:T(128)}, bf16[4,256,1024]{2,1,0:T(8,128)(2,1)}, bf16[4,256,512]{2,1,0:T(8,128)(2,1)}, bf16[4,256,100]{2,1,0:T(8,128)(2,1)S(1)}, bf16[100,102...) while((s32[]{:T(128)}, bf16[4,256,1024]{2,1,0:T(8,128)(2,1)}, ...), condition=%wide.region_5.6_spmd, body=%wide.region_2.0_spmd.sunk | while | flops 323617024 | bytes 6320209 | solution.py:94
  34.8 1.2 fusion.140
  37.0 1.3 fusion.102
  38.5 1.4 bitcast_reduce_fusion.1
  44.9 1.7 copy.44
  46.7 5.7 %convert_reduce_fusion = f32[256,256]{1,0:T(8,128)S(1)} fusion(s32[256,32]{1,0:T(8,128)S(1)} %copy.46), kind=kLoop, calls=%fused_computation.14 | loop fusion | flops 6225920 | bytes 294912 | tf_op jit(solution)/shard_map/reduce_sum | solution.py:139
  53.2 1.5 convolution_convert_fusion.10
  54.8 29.2 %all-reduce.3.cloned.1.call-done = bf16[256,1024]{1,0:T(8,128)(2,1)} async-done(((bf16[256,1024]{1,0:T(8,128)(2,1)}), bf16[256,1024]{1,0:T(8,128)(2,1)}) %all-reduce.3.cloned.1.call-update) | async-done | bytes 524304 | tf_op jit(solution)/shard_map/psum | solution.py:123
  83.9 1.3 fusion.89
  85.3 1.3 multiply_reduce_fusion.1
  88.6 1.7 copy.48
  91.1 1.3 fusion.105
  92.5 3.2 %fusion.42 = (f32[4,256]{1,0:T(4,128)}, f32[4,256,256]{1,2,0:T(8,128)}) fusion(f32[256,256]{0,1:T(8,128)} %copy.47, bf16[256,4,64]{0,2,1:T(8,128)(2,1)} %bitcast.130, bf16[256,4,64]{0,2,1:T(8,128)(2,1)} %bitcast.132), kind=kOutput, calls=%fused_computation.83 | convolution fusion | flops 34601984 | bytes 1576960 | tf_op jit(solution)/shard_map/ihd,jhd->hij/dot_general | solution.py:146
  95.6 3.1 %convolution_convert_fusion.9 = bf16[4,64,256]{2,1,0:T(8,128)(2,1)S(1)} fusion(bf16[256,4,64]{0,2,1:T(8,128)(2,1)} %bitcast.133, f32[4,256,256]{1,2,0:T(8,128)} %fusion.105, f32[4,256,256]{1,2,0:T(8,128)} %get-tuple-element.69, f32[4,256]{1,0:T(4,128)} %get-tuple-element.68, f32[256,256]{0,1:T(8,128)} %copy.47), kind=kOutput, calls=%fused_computation.44 | convolution fusion | flops 37291264 | bytes 2625536 | tf_op jit(solution)/shard_map/hij,jhd->ihd/dot_general | solution.py:172
  98.8 3.8 %convolution_convert_fusion.8 = bf16[4,64,256]{2,1,0:T(8,128)(2,1)} fusion(bf16[256,4,64]{0,2,1:T(8,128)(2,1)} %bitcast.131, f32[4,256,256]{1,2,0:T(8,128)} %fusion.105, f32[4,256,256]{1,2,0:T(8,128)} %get-tuple-element.69, f32[4,256]{1,0:T(4,128)} %get-tuple-element.68, f32[256,256]{0,1:T(8,128)} %copy.47), kind=kOutput, calls=%fused_computation.43 | convolution fusion | flops 37291264 | bytes 2625536 | tf_op jit(solution)/shard_map/hij,ihd->jhd/dot_general | solution.py:175
  102.6 1.6 convolution_convert_fusion.7
  104.2 1.4 convolution_convert_fusion.3
  105.7 1.7 convolution_convert_fusion.11
  108.6 35.5 %all-reduce.5.cloned.1.call-done = bf16[256,1024]{1,0:T(8,128)(2,1)} async-done(((bf16[256,1024]{1,0:T(8,128)(2,1)}), bf16[256,1024]{1,0:T(8,128)(2,1)}) %all-reduce.5.cloned.1.call-update) | async-done | bytes 524304 | tf_op jit(solution)/shard_map/psum | solution.py:186
  144.1 1.6 convert_reduce_fusion.1
  145.8 1.7 fusion.69
  150.1 2.9 %fusion.27 = f32[1024,512]{1,0:T(8,128)S(1)} fusion(bf16[1024,1024]{1,0:T(8,128)(2,1)} %bitcast.20, bf16[1024,256]{0,1:T(8,128)(2,1)S(1)} %get-tuple-element.70, bf16[1024,256]{0,1:T(8,128)(2,1)S(1)} %fusion.31), kind=kOutput, calls=%fused_computation.64 | convolution fusion | flops 1075838976 | bytes 5242880 | tf_op jit(solution)/shard_map/dot_general | solution.py:223
  153.1 1.6 add_convert_fusion
  154.7 13.9 %reduce-scatter.3.cloned.1.call-done = bf16[256,256]{1,0:T(8,128)(2,1)} async-done(((bf16[256,1024]{1,0:T(8,128)(2,1)}), bf16[256,256]{1,0:T(8,128)(2,1)}) %reduce-scatter.3.cloned.1.call-update) | async-done | bytes 131088 | tf_op jit(solution)/shard_map/reduce_scatter | solution.py:160
  168.6 1.6 add_convert_fusion.1
  170.2 23.9 %reduce-scatter.5.cloned.1.call-done = bf16[256,512]{1,0:T(8,128)(2,1)} async-done(((bf16[1024,512]{1,0:T(8,128)(2,1)}), bf16[256,512]{1,0:T(8,128)(2,1)}) %reduce-scatter.5.cloned.1.call-update) | async-done | bytes 262160 | tf_op jit(solution)/shard_map/reduce_scatter | solution.py:224
  194.2 2.1 %reshape.203 = f32[256,2,256]{2,1,0:T(2,128)} reshape(bf16[256,512]{1,0:T(8,128)(2,1)} %reduce-scatter.5.cloned.1.call-done) | data formatting | bytes 786432 | tf_op jit(solution)/shard_map/reshape | solution.py:233
  (152 shorter events, 28.2 us)
Async XLA Ops:
  7.2 36.3 %copy-start = (bf16[256,1024]{1,0:T(8,128)(2,1)S(1)}, bf16[256,1024]{1,0:T(8,128)(2,1)}, u32[]{:S(2)}) copy-start(bf16[256,1024]{1,0:T(8,128)(2,1)} %param.20) | copy-start | bytes 1572868
  8.5 10.8 %copy-start.1 = (bf16[256,1024]{1,0:T(8,128)(2,1)S(1)}, bf16[256,1024]{1,0:T(8,128)(2,1)}, u32[]{:S(2)}) copy-start(bf16[256,1024]{1,0:T(8,128)(2,1)} %param.16) | copy-start | bytes 1572868
  10.1 9.7 %copy-start.7 = (bf16[1024,2,256]{2,1,0:T(2,128)(2,1)S(1)}, bf16[1024,2,256]{2,1,0:T(2,128)(2,1)}, u32[]{:S(2)}) copy-start(bf16[1024,2,256]{2,1,0:T(2,128)(2,1)} %param.19) | copy-start | bytes 3145732
  14.3 5.7 %copy-start.29 = (s32[1,4,256]{2,1,0:T(4,128)S(1)}, s32[1,4,256]{2,1,0:T(4,128)}, u32[]{:S(2)}) copy-start(s32[1,4,256]{2,1,0:T(4,128)} %param.24) | copy-start | bytes 12292
  14.3 5.7 %copy-start.30 = (s32[1,4]{1,0:T(1,128)S(1)}, s32[1,4]{1,0:T(1,128)}, u32[]{:S(2)}) copy-start(s32[1,4]{1,0:T(1,128)} %param.25) | copy-start | bytes 52
  15.1 9.7 %all-to-all-start = ((bf16[4,8,3200]{2,1,0:T(8,128)(2,1)}), bf16[4,8,3200]{2,1,0:T(8,128)(2,1)S(1)}, u32[]{:S(2)}, u32[]{:S(2)}) async-start(bf16[4,8,3200]{2,1,0:T(8,128)(2,1)} %broadcast_select_fusion), calls=%async_computation | async-start | bytes 409600 | tf_op jit(solution)/shard_map/all_to_all | solution.py:82
  19.3 64.6 %all-reduce.3.cloned.1.call-start = ((), (), s32[]{:S(2)}) async-start(), calls=%async_computation.3 | async-start | bytes 1048576 | tf_op jit(solution)/shard_map/psum | solution.py:123
  20.0 22.6 %copy-start.14 = (s32[1,2,4,128]{3,1,2,0:T(2,128)}, s32[1,2,4,128]{3,1,2,0:T(2,128)S(1)}, u32[]{:S(2)}) copy-start(s32[1,2,4,128]{3,1,2,0:T(2,128)S(1)} %copy.62) | copy-start | bytes 12292
  20.1 5.6 %copy-start.2 = (bf16[100,1024]{1,0:T(8,128)(2,1)S(1)}, bf16[100,1024]{1,0:T(8,128)(2,1)}, u32[]{:S(2)}) copy-start(bf16[100,1024]{1,0:T(8,128)(2,1)} %param.17) | copy-start | bytes 614404
  20.8 4.9 %copy-start.9 = (bf16[256,512]{0,1:T(8,128)(2,1)}, bf16[256,512]{0,1:T(8,128)(2,1)S(1)}, u32[]{:S(2)}) copy-start(bf16[256,512]{0,1:T(8,128)(2,1)S(1)} %convolution_convert_fusion.5) | copy-start | bytes 786436
  22.4 16.1 %copy-start.11 = (bf16[256,256]{0,1:T(8,128)(2,1)}, bf16[256,256]{0,1:T(8,128)(2,1)S(1)}, u32[]{:S(2)}) copy-start(bf16[256,256]{0,1:T(8,128)(2,1)S(1)} %get-tuple-element.64) | copy-start | bytes 393220
  22.4 17.6 %copy-start.33 = (f32[256,4]{0,1:T(4,128)}, f32[256,4]{0,1:T(4,128)S(1)}, u32[]{:S(2)}) copy-start(f32[256,4]{0,1:T(4,128)S(1)} %get-tuple-element.63) | copy-start | bytes 12292
  39.9 3.5 %copy-start.19 = (f32[1024,4]{0,1:T(4,128)}, f32[1024,4]{0,1:T(4,128)S(1)}, u32[]{:S(2)}) copy-start(f32[1024,4]{0,1:T(4,128)S(1)} %get-tuple-element.61) | copy-start | bytes 49156
  39.9 2.7 %slice-start = ((bf16[256,512]{0,1:T(8,128)(2,1)}), bf16[256,256]{0,1:T(8,128)(2,1)S(1)}, s32[]{:S(2)}) async-start(bf16[256,512]{0,1:T(8,128)(2,1)} %copy-done.9), calls=%async_computation.7 | async-start | bytes 262144 | tf_op jit(solution)/shard_map/slice | solution.py:104
  42.5 2.1 %copy-start.16 = (f32[256,4]{0,1:T(4,128)}, f32[256,4]{0,1:T(4,128)S(1)}, u32[]{:S(2)}) copy-start(f32[256,4]{0,1:T(4,128)S(1)} %convert_element_type.158) | copy-start | bytes 12292
  44.6 2.0 copy-start.18
  44.6 99.5 %all-reduce.5.cloned.1.call-start = ((), (), s32[]{:S(2)}) async-start(), calls=%async_computation.5 | async-start | bytes 1048576 | tf_op jit(solution)/shard_map/psum | solution.py:186
  83.9 3.3 %copy-start.3 = (bf16[256,1024]{1,0:T(8,128)(2,1)S(1)}, bf16[256,1024]{1,0:T(8,128)(2,1)}, u32[]{:S(2)}) copy-start(bf16[256,1024]{1,0:T(8,128)(2,1)} %all-reduce.3.cloned.1.call-done) | copy-start | bytes 1572868
  105.7 1.8 copy-start.6
  105.7 38.4 %copy-start.4 = (bf16[256,1024]{1,0:T(8,128)(2,1)S(1)}, bf16[256,1024]{1,0:T(8,128)(2,1)}, u32[]{:S(2)}) copy-start(bf16[256,1024]{1,0:T(8,128)(2,1)} %all-reduce.3.cloned.1.call-done) | copy-start | bytes 1572868
  105.7 62.9 %reduce-scatter.3.cloned.1.call-start = ((), (), s32[]{:S(2)}) async-start(), calls=%async_computation.4 | async-start | bytes 655360 | tf_op jit(solution)/shard_map/reduce_scatter | solution.py:160
  107.4 38.3 %copy-start.10 = (bf16[256,512]{0,1:T(8,128)(2,1)S(1)}, bf16[256,512]{0,1:T(8,128)(2,1)}, u32[]{:S(2)}) copy-start(bf16[256,512]{0,1:T(8,128)(2,1)} %copy-done.9) | copy-start | bytes 786436
  108.6 37.2 %copy-start.22 = (f32[256]{0:T(256)S(1)}, f32[256]{0:T(256)}, u32[]{:S(2)}) copy-start(f32[256]{0:T(256)} %copy-done.21) | copy-start | bytes 3076
  108.6 37.2 %copy-start.26 = (f32[256]{0:T(256)S(1)}, f32[256]{0:T(256)}, u32[]{:S(2)}) copy-start(f32[256]{0:T(256)} %copy-done.25) | copy-start | bytes 3076
  108.6 85.6 %reduce-scatter.5.cloned.1.call-start = ((), (), s32[]{:S(2)}) async-start(), calls=%async_computation.6 | async-start | bytes 1310720 | tf_op jit(solution)/shard_map/reduce_scatter | solution.py:224
  145.7 1.9 copy-start.17
  145.7 1.8 copy-start.15
  147.5 1.8 copy-start.12
  147.5 1.8 copy-start.20
  147.6 2.4 %copy-start.5 = (f32[1024,256]{0,1:T(8,128)S(1)}, f32[1024,256]{0,1:T(8,128)}, u32[]{:S(2)}) copy-start(f32[1024,256]{0,1:T(8,128)} %get-tuple-element.62) | copy-start | bytes 3145732
  150.1 2.9 %copy-start.24 = (f32[256]{0:T(256)S(1)}, f32[256]{0:T(256)}, u32[]{:S(2)}) copy-start(f32[256]{0:T(256)} %copy-done.23) | copy-start | bytes 3076
  150.1 2.9 %copy-start.28 = (f32[256]{0:T(256)S(1)}, f32[256]{0:T(256)}, u32[]{:S(2)}) copy-start(f32[256]{0:T(256)} %copy-done.27) | copy-start | bytes 3076
  (10 other events, 13.0 us)
Sparse Core Ops, SparseCore 0:
  44.7 39.1 all-reduce.2
  105.8 38.2 all-reduce.4
  147.0 21.6 reduce-scatter.2
  171.0 23.1 reduce-scatter.4
where the time goes:
time: 203 us
  waiting for transfers between devices  105 us (52%)
  matrix products  42 us (21%)
  local copies, waits for them, and re-layouts  18.6 us (9%)
  other arithmetic  18.2 us (9%)
  between operations  14.5 us (7%)
  starting transfers between devices  4.54 us (2%)
    psum x1, waiting for transfers between devices, body(): lax.psum(d_part.astype(jnp.bfloat16), 'head').astype(jnp.float32)  35.5 us
    psum x1, waiting for transfers between devices, body(): lax.psum(enc_part.astype(jnp.bfloat16), 'head').astype(jnp.float32)  29.2 us
    reduce_scatter x1, waiting for transfers between devices, body(): lax.psum_scatter((total + lax.dot_general(mesh_normed, self_grad, dims, p...  23.9 us
    reduce_scatter x1, waiting for transfers between devices, body(): lax.psum_scatter(out_part.astype(jnp.bfloat16), 'head', scatter_dimension...  13.9 us
    reduce_sum x1, other arithmetic, body(): jnp.sum((win_idx[:, :, None] == lax.broadcasted_iota(jnp.int32, (1, 1, me...  5.69 us
    unnamed x81, local copies, waits for them, and re-layouts  5.23 us
    dot_general x4, matrix products, one_source(): jnp.dot(normed, kv_flat, preferred_element_type=float_value)  4.84 us
    dot_general x4, matrix products, slot_rows(): jnp.dot(onehot, flat, precision=highest, preferred_element_type=jnp.float32)  4.28 us
  transfers between devices with their start and end apart: 5, of which 5 were waited for; matrix products, arithmetic and copies ran while one was open for 14% of the time, Pallas kernels for 0%

commit v1 on v0

v1 whole, which is shorter than its diff:
```python
import functools
import math

import jax
import jax.numpy as jnp
from jax import lax
from jax.experimental import pallas as pl
from jax.experimental.pallas import tpu as pltpu
from jax.sharding import PartitionSpec as P

HEAD_SIZE = 64
LANES = 128

norm_eps = 1e-05
cap_limit = 30.0
scale = 1.0 / math.sqrt(HEAD_SIZE)

f32 = jnp.float32
bf16 = jnp.bfloat16
MESH = pl.DeviceIdType.MESH


def normalize(values):
    row_mean = jnp.mean(values, axis=-1, keepdims=True)
    centred = values - row_mean
    var = jnp.mean(centred * centred, axis=-1, keepdims=True)
    inv = lax.rsqrt(var + norm_eps)
    return centred * inv, inv


def dot(a, b):
    return jnp.dot(a, b, preferred_element_type=f32)


def dot_t(a, b):
    return lax.dot_general(a, b, (((1,), (1,)), ((), ())), preferred_element_type=f32)


def t_dot(a, b):
    return lax.dot_general(a, b, (((0,), (0,)), ((), ())), preferred_element_type=f32)


def split(x):
    hi = x.astype(bf16)
    return hi, (x - hi.astype(f32)).astype(bf16)


def dot_split(a, x):
    hi, lo = split(x)
    return dot(a, hi) + dot(a, lo)


def kernel(
    n_grid,
    n_head,
    gx_ref,
    mesh_ref,
    w_in_ref,
    w_q_ref,
    w_kv_ref,
    w_o_ref,
    w_pqkv_ref,
    w_po_ref,
    src_ref,
    dst_ref,
    win_ref,
    cot_ref,
    hm_ref,
    grad_ref,
    rows_t,
    x_t,
    hot,
    hot_t,
    kv,
    tanh_e,
    prob_e,
    grads,
    q_s,
    kv_s,
    members,
    enc_send,
    enc_recv,
    normed,
    out_send,
    out_recv,
    hm_rows,
    hm_cols,
    back_send,
    back_recv,
    d_hm,
    grad_send,
    grad_recv,
    hs_sem,
    hr_sem,
    gs_sem,
    gr_sem,
):
    width = mesh_ref.shape[1]
    nodes = mesh_ref.shape[0]
    cols = w_q_ref.shape[1]
    cap = src_ref.shape[2]
    heads = cols // HEAD_SIZE
    own = nodes // n_head
    chunk = width // n_grid
    my_grid = lax.axis_index("grid")
    my_head = lax.axis_index("head")
    grid_peers = [lax.rem(my_grid + d, n_grid) for d in range(1, n_grid)]
    head_peers = [lax.rem(my_head + d, n_head) for d in range(1, n_head)]

    barrier = pltpu.get_barrier_semaphore()
    for peer in grid_peers:
        pl.semaphore_signal(barrier, inc=1, device_id={"grid": peer}, device_id_type=MESH)
    for peer in head_peers:
        pl.semaphore_signal(barrier, inc=1, device_id={"head": peer}, device_id_type=MESH)

    def send_grid(phase, d, src, dst):
        c = pltpu.make_async_remote_copy(
            src_ref=src,
            dst_ref=dst,
            send_sem=gs_sem.at[phase, d],
            recv_sem=gr_sem.at[phase, d],
            device_id={"grid": grid_peers[d]},
            device_id_type=MESH,
        )
        c.start()
        return c

    def send_head(phase, d, src, dst):
        c = pltpu.make_async_remote_copy(
            src_ref=src,
            dst_ref=dst,
            send_sem=hs_sem.at[phase, d],
            recv_sem=hr_sem.at[phase, d],
            device_id={"head": head_peers[d]},
            device_id_type=MESH,
        )
        c.start()
        return c

    def head_rows(peer):
        return pl.ds(pl.multiple_of(peer * own, own), own)

    def grid_rows(peer):
        return pl.ds(pl.multiple_of(peer * chunk, chunk), chunk)

    own_rows = head_rows(my_head)
    copies = []

    def gathered(peer):
        idx = src_ref[peer]
        total = None
        rows = gx_ref.shape[1]
        step = 512
        for start in range(0, rows, step):
            at = lax.broadcasted_iota(jnp.int32, (step, cap), 0) + start
            pick = jnp.where(at == idx, 1.0, 0.0).astype(bf16)
            part = dot(gx_ref[:, start : start + step], pick)
            total = part if total is None else total + part
        return total.astype(bf16)

    rows_t[n_grid] = gathered(grid_peers[0])
    pl.semaphore_wait(barrier, n_grid - 1 + n_head - 1)
    edge_copies = [send_grid(0, 0, rows_t.at[n_grid], rows_t.at[my_grid])]
    for d in range(1, n_grid - 1):
        rows_t[n_grid + d] = gathered(grid_peers[d])
        edge_copies.append(send_grid(0, d, rows_t.at[n_grid + d], rows_t.at[my_grid]))
    rows_t[my_grid] = gathered(my_grid)
    copies += edge_copies

    mesh_f = mesh_ref[...].astype(f32)
    mesh_n = normalize(mesh_f)[0]
    x_t[:, n_grid * cap : n_grid * cap + nodes] = mesh_n.T.astype(bf16)
    mesh_n = mesh_n.astype(bf16)
    q_s[...] = dot(mesh_n, w_q_ref[...]).astype(bf16)
    kv_s[...] = dot(mesh_n, w_kv_ref[...]).astype(bf16)

    def onehots(s, carry):
        at = lax.broadcasted_iota(jnp.int32, (nodes, cap), 0)
        pick = jnp.where(at == dst_ref[s], 1.0, 0.0)
        hot_t[s] = pick.astype(bf16)
        hot[s] = pick.T.astype(bf16)
        return carry

    lax.fori_loop(0, n_grid, onehots, 0)

    row_at = lax.shift_right_logical(lax.broadcasted_iota(jnp.int32, (cols, cols), 0), 6)
    col_at = lax.shift_right_logical(lax.broadcasted_iota(jnp.int32, (cols, cols), 1), 6)
    same_head = jnp.where(row_at == col_at, 1.0, 0.0).astype(bf16)

    def head_sum(x):
        hi, lo = split(x)
        return dot(hi, same_head) + dot(lo, same_head)

    for c in edge_copies:
        c.wait_recv()

    def embed(s, carry):
        row = normalize(t_dot(rows_t[s], w_in_ref[...]))[0]
        x_t[:, pl.ds(pl.multiple_of(s * cap, cap), cap)] = row.T.astype(bf16)
        kv[s] = dot(row.astype(bf16), w_kv_ref[...]).astype(bf16)
        return carry

    lax.fori_loop(0, n_grid, embed, 0)

    query = q_s[...]
    q_f = query.astype(f32)
    k_f = kv_s[:, :cols].astype(f32)
    v_f = kv_s[:, cols:].astype(f32)
    tanh_s = jnp.tanh(head_sum(q_f * k_f) * (scale / cap_limit))
    weight_s = jnp.exp(cap_limit * tanh_s)

    def scores(s, denom):
        q_e = dot(hot[s], query)
        t = jnp.tanh(head_sum(q_e * kv[s][:, :cols].astype(f32)) * (scale / cap_limit))
        w = jnp.exp(cap_limit * t)
        tanh_e[s] = t
        prob_e[s] = w
        return denom + dot_split(hot_t[s], w)

    denom = lax.fori_loop(0, n_grid, scores, weight_s)
    recip = 1.0 / denom
    prob_s = weight_s * recip
    recip_hi, recip_lo = split(recip)
    ps_b = prob_s.astype(bf16)

    def mix(s, total):
        p = prob_e[s] * (dot(hot[s], recip_hi) + dot(hot[s], recip_lo))
        prob_e[s] = p
        v = kv[s][:, cols:].astype(f32)
        return total + dot_split(hot_t[s], p.astype(bf16).astype(f32) * v)

    mixed = lax.fori_loop(0, n_grid, mix, ps_b.astype(f32) * v_f).astype(bf16)
    enc_send[...] = dot(mixed, w_o_ref[...]).astype(bf16)
    enc_copies = [
        send_head(0, d, enc_send.at[head_rows(head_peers[d])], enc_recv.at[d])
        for d in range(n_head - 1)
    ]
    copies += enc_copies

    lane = lax.broadcasted_iota(jnp.int32, (nodes, nodes), 1)
    win = win_ref[...]
    count = jnp.zeros((nodes, nodes), f32)
    for m in range(win.shape[1]):
        count = count + jnp.where(lane == win[:, m : m + 1], 1.0, 0.0)
    members[...] = count
    d_att = dot_t(cot_ref[...], w_po_ref[...]).astype(bf16)

    for c in enc_copies:
        c.wait_recv()
    enc_sum = enc_send[own_rows].astype(f32)
    for d in range(n_head - 1):
        enc_sum = enc_sum + enc_recv[d].astype(f32)
    hm1 = mesh_ref[own_rows].astype(f32) + enc_sum
    xhat, inv = normalize(hm1)
    normed[own_rows] = xhat.astype(bf16)
    norm_copies = [
        send_head(1, d, normed.at[own_rows], normed.at[own_rows]) for d in range(n_head - 1)
    ]
    copies += norm_copies
    for c in norm_copies:
        c.wait_recv()

    qkv = dot(normed[...], w_pqkv_ref[...]).astype(bf16)
    q2 = qkv[:, :cols]
    k2 = qkv[:, cols : 2 * cols]
    v2 = qkv[:, 2 * cols :]
    col_head = lax.shift_right_logical(lax.broadcasted_iota(jnp.int32, (nodes, cols), 1), 6)
    zero = jnp.zeros((nodes, cols), f32)
    attended, d_q, d_k, d_v = zero, zero, zero, zero
    for h in range(heads):
        mine = col_head == h
        q_h = jnp.where(mine, q2.astype(f32), 0.0).astype(bf16)
        a_h = jnp.where(mine, d_att.astype(f32), 0.0).astype(bf16)
        tanh2 = jnp.tanh(dot_t(q_h, k2) * (scale / cap_limit))
        weight2 = members[...] * jnp.exp(cap_limit * tanh2)
        prob2 = weight2 / jnp.sum(weight2, axis=1, keepdims=True)
        pb = prob2.astype(bf16)
        attended = jnp.where(mine, dot(pb, v2), attended)
        dprob = dot_t(a_h, v2)
        ds = prob2 * (dprob - jnp.sum(prob2 * dprob, axis=1, keepdims=True))
        dz = ds * (1.0 - tanh2 * tanh2) * scale
        d_q = jnp.where(mine, dot(dz.astype(bf16), k2), d_q)
        d_k = jnp.where(mine, dot(dz.T.astype(bf16), q2), d_k)
        d_v = jnp.where(mine, dot(prob2.T.astype(bf16), d_att), d_v)
    back = dot_t(d_q.astype(bf16), w_pqkv_ref[:, :cols])
    back = back + dot_t(d_k.astype(bf16), w_pqkv_ref[:, cols : 2 * cols])
    back = back + dot_t(d_v.astype(bf16), w_pqkv_ref[:, 2 * cols :])
    back_send[...] = back.astype(bf16)
    back_copies = [
        send_head(2, d, back_send.at[head_rows(head_peers[d])], back_recv.at[d])
        for d in range(n_head - 1)
    ]
    copies += back_copies
    out_send[...] = dot(attended.astype(bf16), w_po_ref[...]).astype(bf16)
    for c in back_copies:
        c.wait_recv()
    d_n = back_send[own_rows].astype(f32)
    for d in range(n_head - 1):
        d_n = d_n + back_recv[d].astype(f32)
    d_n = d_n - jnp.mean(d_n, axis=1, keepdims=True) - xhat * jnp.mean(d_n * xhat, axis=1, keepdims=True)
    d_hm[own_rows] = (cot_ref[own_rows].astype(f32) + inv * d_n).astype(bf16)
    d_hm_copies = [
        send_head(3, d, d_hm.at[own_rows], d_hm.at[own_rows]) for d in range(n_head - 1)
    ]
    out_copies = [
        send_head(4, d, out_send.at[head_rows(head_peers[d])], out_recv.at[d])
        for d in range(n_head - 1)
    ]
    copies += d_hm_copies + out_copies
    for c in d_hm_copies:
        c.wait_recv()

    d_mixed = dot_t(d_hm[...], w_o_ref[...]).astype(bf16)
    dm_f = d_mixed.astype(f32)
    dprob_s = head_sum(dm_f * v_f)

    def inners(s, total):
        dprob = head_sum(dot(hot[s], d_mixed) * kv[s][:, cols:].astype(f32))
        return total + dot_split(hot_t[s], prob_e[s] * dprob)

    inner = lax.fori_loop(0, n_grid, inners, prob_s * dprob_s)
    in_hi, in_lo = split(inner)

    def edge_grads(s, carry):
        h = hot[s]
        q_e = dot(h, query)
        dm_e = dot(h, d_mixed)
        dprob = head_sum(dm_e * kv[s][:, cols:].astype(f32))
        t = tanh_e[s]
        p = prob_e[s]
        dz = p * (dprob - (dot(h, in_hi) + dot(h, in_lo))) * (1.0 - t * t) * scale
        at = pl.ds(pl.multiple_of(s * cap, cap), cap)
        grads[at, :cols] = (dz * q_e).astype(bf16)
        grads[at, cols:] = (p.astype(bf16).astype(f32) * dm_e).astype(bf16)
        return carry

    lax.fori_loop(0, n_grid, edge_grads, 0)
    dz_s = prob_s * (dprob_s - inner) * (1.0 - tanh_s * tanh_s) * scale
    grads[n_grid * cap : n_grid * cap + nodes, :cols] = (dz_s * q_f).astype(bf16)
    grads[n_grid * cap : n_grid * cap + nodes, cols:] = (ps_b.astype(f32) * dm_f).astype(bf16)

    grad_copies = []
    for d in range(n_grid - 1):
        rows = grid_rows(grid_peers[d])
        grad_send[d] = dot(x_t[rows], grads[...]).astype(bf16)
        grad_copies.append(send_grid(1, d, grad_send.at[d], grad_recv.at[d]))
    copies += grad_copies
    grad_own = dot(x_t[grid_rows(my_grid)], grads[...])

    for c in out_copies:
        c.wait_recv()
    out_sum = out_send[own_rows].astype(f32)
    for d in range(n_head - 1):
        out_sum = out_sum + out_recv[d].astype(f32)
    hm_rows[...] = (hm1 + out_sum).astype(bf16)
    def head_cols(peer):
        return pl.ds(pl.multiple_of(peer * cols, cols), cols)

    col_copies = [
        send_head(5, d, hm_rows.at[:, head_cols(head_peers[d])], hm_cols.at[own_rows])
        for d in range(n_head - 1)
    ]
    copies += col_copies
    hm_cols[own_rows] = hm_rows[:, head_cols(my_head)]
    for c in col_copies:
        c.wait_recv()
    hm_ref[...] = hm_cols[...]

    for c in grad_copies:
        c.wait_recv()
    for d in range(n_grid - 1):
        grad_own = grad_own + grad_recv[d].astype(f32)
    grad_ref[...] = grad_own
    for c in copies:
        c.wait_send()


def body(
    grid_x, mesh_h, w_in, w_q, w_kv, w_o, w_pqkv, w_po, edge_src, edge_dst, edge_count, win_idx, cot
):
    n_grid = lax.axis_size("grid")
    n_head = lax.axis_size("head")
    cols = w_q.shape[1]
    nodes, width = mesh_h.shape
    cap = edge_src.shape[2]
    channels = grid_x.shape[1]
    own = nodes // n_head
    chunk = width // n_grid
    slots = n_grid * cap
    heads = cols // HEAD_SIZE
    pad = -channels % LANES
    gx = jnp.pad(grid_x.T, ((0, pad), (0, 0)))
    w_in_p = jnp.pad(w_in, ((0, pad), (0, 0)))
    live = lax.broadcasted_iota(jnp.int32, (n_grid, cap), 1) < edge_count[0][:, None]
    dst = jnp.where(live, edge_dst[0], -1).reshape(n_grid, 1, cap)
    src = edge_src[0].reshape(n_grid, 1, cap)
    vmem = pl.BlockSpec(memory_space=pltpu.VMEM)
    hm, grad = pl.pallas_call(
        functools.partial(kernel, n_grid, n_head),
        out_shape=(
            jax.ShapeDtypeStruct((nodes, cols), bf16),
            jax.ShapeDtypeStruct((chunk, 2 * cols), f32),
        ),
        in_specs=[vmem] * 12,
        out_specs=(vmem, vmem),
        scratch_shapes=[
            pltpu.VMEM((2 * n_grid - 1, channels + pad, cap), bf16),
            pltpu.VMEM((width, slots + nodes), bf16),
            pltpu.VMEM((n_grid, cap, nodes), bf16),
            pltpu.VMEM((n_grid, nodes, cap), bf16),
            pltpu.VMEM((n_grid, cap, 2 * cols), bf16),
            pltpu.VMEM((n_grid, cap, cols), f32),
            pltpu.VMEM((n_grid, cap, cols), f32),
            pltpu.VMEM((slots + nodes, 2 * cols), bf16),
            pltpu.VMEM((nodes, cols), bf16),
            pltpu.VMEM((nodes, 2 * cols), bf16),
            pltpu.VMEM((nodes, nodes), f32),
            pltpu.VMEM((nodes, width), bf16),
            pltpu.VMEM((n_head - 1, own, width), bf16),
            pltpu.VMEM((nodes, width), bf16),
            pltpu.VMEM((nodes, width), bf16),
            pltpu.VMEM((n_head - 1, own, width), bf16),
            pltpu.VMEM((own, width), bf16),
            pltpu.VMEM((nodes, cols), bf16),
            pltpu.VMEM((nodes, width), bf16),
            pltpu.VMEM((n_head - 1, own, width), bf16),
            pltpu.VMEM((nodes, width), bf16),
            pltpu.VMEM((n_grid - 1, chunk, 2 * cols), bf16),
            pltpu.VMEM((n_grid - 1, chunk, 2 * cols), bf16),
            pltpu.SemaphoreType.DMA((6, n_head - 1)),
            pltpu.SemaphoreType.DMA((6, n_head - 1)),
            pltpu.SemaphoreType.DMA((2, n_grid - 1)),
            pltpu.SemaphoreType.DMA((2, n_grid - 1)),
        ],
        compiler_params=pltpu.CompilerParams(
            collective_id=0, has_side_effects=True, vmem_limit_bytes=56 * 1024 * 1024
        ),
    )(
        gx,
        mesh_h,
        w_in_p,
        w_q,
        w_kv.reshape(width, 2 * cols),
        w_o,
        w_pqkv.reshape(width, 3 * cols),
        w_po,
        src,
        dst,
        win_idx,
        cot,
    )
    return hm, grad.reshape(chunk, 2, cols)


def solution(mesh):
    placed = (
        P(("groups", "grid"), None),
        P(("groups", "grid"), None),
        P(),
        P(None, "head"),
        P(None, None, "head"),
        P("head", None),
        P(None, None, "head"),
        P("head", None),
        P("grid", None, None),
        P("grid", None, None),
        P("grid", None),
        P("grid", None),
        P(("groups", "grid"), None),
    )
    return jax.shard_map(
        body,
        mesh=mesh,
        in_specs=placed,
        out_specs=(P(("groups", "grid"), "head"), P(("groups", "grid"), None, "head")),
        check_vma=False,
    )
```

time: 203 us -> 108 us (0.53)
  the two profiles are of different devices: /device:TPU:0 before, /device:TPU:29 now
where the time goes in v1:
time: 108 us
  Pallas kernels  95.5 us (88%)
  local copies, waits for them, and re-layouts  11.2 us (10%)
    pallas_call x1, Pallas kernels, body(): pl.pallas_call(functools.partial(kernel, n_grid, n_head), out_shape=(jax....  95.5 us
    unnamed x18, local copies, waits for them, and re-layouts  5.28 us
    reshape x1, local copies, waits for them, and re-layouts, body(): return (hm, grad.reshape(chunk, 2, cols))  2.16 us

profile of v1, /device:TPU:29, one launch (start us, length us, event | category | flops | bytes accessed | tf_op | source)
XLA Modules:
  0.0 108.0 jit_solution(795899604661757815)
XLA Ops:
  0.6 1.7 %copy.17 = bf16[1024,3,256]{0,2,1:T(8,128)(2,1)S(1)} copy(bf16[1024,3,256]{2,0,1:T(8,128)(2,1)} %param.19) | data formatting | bytes 3145728 | tf_op args[6]
  2.4 0.0 copy-start
  2.4 1.6 %copy.18.w_pqkv_ref = bf16[1024,768]{1,0:T(8,128)(2,1)} copy(bf16[1024,768]{0,1:T(8,128)(2,1)S(1)} %bitcast.5) | data formatting | bytes 3145728 | tf_op jit(solution)/shard_map/reshape | solution.py:445
  4.0 0.0 copy-start.1
  4.0 0.0 copy-start.2
  4.0 0.0 copy-done
  4.0 0.0 copy-start.3
  4.0 0.0 copy-start.4
  4.0 0.0 copy-start.6
  4.0 0.0 copy-start.5
  4.0 1.2 %copy.20 = bf16[128,8,2,256]{3,1,2,0:T(8,128)(2,1)} copy(bf16[128,8,2,256]{3,2,1,0:T(2,128)(2,1)S(1)} %bitcast.7) | data formatting | bytes 2097152
  5.2 0.0 copy-done.1
  5.2 0.8 pad.8.gx_ref
  6.1 0.0 copy-done.2
  6.1 0.7 pad.9.w_in_ref
  6.8 0.0 copy-done.3
  6.8 0.8 copy.19.win_ref
  7.5 0.0 copy-done.4
  7.5 0.0 copy-done.6
  7.6 0.7 compare_select_fusion.dst_ref
  8.2 0.0 copy-done.5
  8.2 0.6 reshape_squeeze.3.src_ref
  8.8 95.5 %shard_map.140 = (bf16[256,256]{1,0:T(8,128)(2,1)}, f32[256,512]{1,0:T(8,128)}) custom-call(bf16[128,2048]{1,0:T(8,128)(2,1)} %pad.8.gx_ref, bf16[256,1024]{1,0:T(8,128)(2,1)} %mesh_ref.1, bf16[128,1024]{1,0:T(8,128)(2,1)} %pad.9.w_in_ref, bf16[1024,256]{1,0:T(8,128)(2,1)} %w_q_ref.1, bf16[1024,512]{1,0:T(8,128)(2,1)} %bitcast.6, bf16[256,1024]{1,0:T(8,128)(2,1)} %w_o_ref.1, ...), custom_call_target="tpu_custom_call" | custom-call | tf_op jit(solution)/shard_map/pallas_call | solution.py:398
  104.3 2.2 %reshape.62 = f32[256,2,256]{2,1,0:T(2,128)} reshape(f32[256,512]{1,0:T(8,128)} %get-tuple-element.5) | data formatting | bytes 1048576 | tf_op jit(solution)/shard_map/reshape | solution.py:452
  106.4 1.6 %copy.22 = bf16[256,256]{1,0:T(8,128)(2,1)} copy(bf16[256,256]{1,0:T(8,128)(2,1)} %get-tuple-element.8) | data formatting | bytes 262144
Async XLA Ops:
  2.4 1.6 %copy-start = (bf16[1024,2,256]{2,1,0:T(2,128)(2,1)S(1)}, bf16[1024,2,256]{2,1,0:T(2,128)(2,1)}, u32[]{:S(2)}) copy-start(bf16[1024,2,256]{2,1,0:T(2,128)(2,1)} %param.17) | copy-start | bytes 3145732
  4.0 1.3 %copy-start.1 = (bf16[2048,100]{0,1:T(8,128)(2,1)S(1)}, bf16[2048,100]{0,1:T(8,128)(2,1)}, u32[]{:S(2)}) copy-start(bf16[2048,100]{0,1:T(8,128)(2,1)} %param.13) | copy-start | bytes 1228804
  4.0 2.1 %copy-start.2 = (bf16[100,1024]{1,0:T(8,128)(2,1)S(1)}, bf16[100,1024]{1,0:T(8,128)(2,1)}, u32[]{:S(2)}) copy-start(bf16[100,1024]{1,0:T(8,128)(2,1)} %param.15) | copy-start | bytes 614404
  4.0 2.8 %copy-start.3 = (s32[256,32]{0,1:T(8,128)S(1)}, s32[256,32]{0,1:T(8,128)}, u32[]{:S(2)}) copy-start(s32[256,32]{0,1:T(8,128)} %param.24) | copy-start | bytes 98308
  4.0 3.6 %copy-start.4 = (s32[1,4,256]{2,1,0:T(4,128)S(1)}, s32[1,4,256]{2,1,0:T(4,128)}, u32[]{:S(2)}) copy-start(s32[1,4,256]{2,1,0:T(4,128)} %param.22) | copy-start | bytes 12292
  4.0 3.6 %copy-start.6 = (s32[1,4]{1,0:T(1,128)S(1)}, s32[1,4]{1,0:T(1,128)}, u32[]{:S(2)}) copy-start(s32[1,4]{1,0:T(1,128)} %param.23) | copy-start | bytes 52
  4.0 4.2 %copy-start.5 = (s32[1,4,256]{2,1,0:T(4,128)S(1)}, s32[1,4,256]{2,1,0:T(4,128)}, u32[]{:S(2)}) copy-start(s32[1,4,256]{2,1,0:T(4,128)} %param.21) | copy-start | bytes 12292

commit v2 on v1

v2 whole, which is shorter than its diff:
```python
import functools
import math

import jax
import jax.numpy as jnp
from jax import lax
from jax.experimental import pallas as pl
from jax.experimental.pallas import tpu as pltpu
from jax.sharding import PartitionSpec as P

HEAD_SIZE = 64

norm_eps = 1e-05
cap_limit = 30.0
scale = 1.0 / math.sqrt(HEAD_SIZE)

f32 = jnp.float32
bf16 = jnp.bfloat16
MESH = pl.DeviceIdType.MESH


def normalize(values):
    row_mean = jnp.mean(values, axis=-1, keepdims=True)
    centred = values - row_mean
    var = jnp.mean(centred * centred, axis=-1, keepdims=True)
    inv = lax.rsqrt(var + norm_eps)
    return centred * inv, inv


def dot(a, b):
    return jnp.dot(a, b, preferred_element_type=f32)


def dot_t(a, b):
    return lax.dot_general(a, b, (((1,), (1,)), ((), ())), preferred_element_type=f32)


def t_dot(a, b):
    return lax.dot_general(a, b, (((0,), (0,)), ((), ())), preferred_element_type=f32)


def split(x):
    hi = x.astype(bf16)
    return hi, (x - hi.astype(f32)).astype(bf16)


def dot_split(a, x):
    hi, lo = split(x)
    return dot(a, hi) + dot(a, lo)


def kernel(
    n_grid,
    n_head,
    n_group,
    gx_ref,
    mesh_ref,
    w_in_ref,
    w_q_ref,
    w_kv_ref,
    w_o_ref,
    w_pqkv_ref,
    w_po_ref,
    src_ref,
    dst_ref,
    count_ref,
    win_ref,
    cot_ref,
    hm_ref,
    grad_ref,
    rows_t,
    x_t,
    hot,
    hot_t,
    kv,
    tanh_e,
    prob_e,
    grads,
    q_s,
    kv_s,
    members,
    w_in_p,
    dst_live,
    wo_full,
    mixed_full,
    hm1_s,
    out_send,
    out_recv,
    back_send,
    back_recv,
    dm_send,
    dm_full,
    pair_send,
    pair_recv,
    grad_send,
    grad_recv,
    hs_sem,
    hr_sem,
    gs_sem,
    gr_sem,
    ws_sem,
    wr_sem,
    xs_sem,
    xr_sem,
    cs_sem,
    cr_sem,
    ps_sem,
    pr_sem,
):
    width = mesh_ref.shape[1]
    nodes = mesh_ref.shape[0]
    cols = w_q_ref.shape[1]
    cap = src_ref.shape[2]
    channels = gx_ref.shape[0]
    padded = w_in_p.shape[0]
    heads = cols // HEAD_SIZE
    own = nodes // n_head
    chunk = width // n_grid
    my_grid = lax.axis_index("grid")
    my_head = lax.axis_index("head")
    my_group = lax.axis_index("groups")
    core = lax.rem(my_grid, 2)
    sibling = my_grid + 1 - 2 * core
    parts = 2 * n_group
    share = cols // parts
    n_pair = n_grid // 2
    my_pair = my_grid // 2
    grid_peers = [lax.rem(my_grid + d, n_grid) for d in range(1, n_grid)]
    head_peers = [lax.rem(my_head + d, n_head) for d in range(1, n_head)]
    head_from = [lax.rem(my_head + n_head - d, n_head) for d in range(1, n_head)]
    group_peers = [lax.rem(my_group + d, n_group) for d in range(1, n_group)]
    group_from = [lax.rem(my_group + n_group - d, n_group) for d in range(1, n_group)]
    pair_peers = [lax.rem(my_pair + d, n_pair) for d in range(1, n_pair)]

    barrier = pltpu.get_barrier_semaphore()
    for peer in grid_peers:
        pl.semaphore_signal(barrier, inc=1, device_id={"grid": peer}, device_id_type=MESH)
    for peer in head_peers:
        pl.semaphore_signal(barrier, inc=1, device_id={"head": peer}, device_id_type=MESH)

    for peer in group_peers:
        pl.semaphore_signal(barrier, inc=1, device_id={"groups": peer}, device_id_type=MESH)

    def send(src, dst, send_sem, recv_sem, to):
        c = pltpu.make_async_remote_copy(
            src_ref=src,
            dst_ref=dst,
            send_sem=send_sem,
            recv_sem=recv_sem,
            device_id=to,
            device_id_type=MESH,
        )
        c.start()
        return c

    def send_grid(phase, d, src, dst):
        to = {"grid": grid_peers[d]}
        return send(src, dst, gs_sem.at[phase, d], gr_sem.at[phase, d], to)

    def send_head(phase, d, src, dst):
        to = {"head": head_peers[d]}
        return send(src, dst, hs_sem.at[phase, d], hr_sem.at[phase, d], to)

    def head_rows(peer):
        return pl.ds(pl.multiple_of(peer * own, own), own)

    def grid_rows(peer):
        return pl.ds(pl.multiple_of(peer * chunk, chunk), chunk)

    def head_cols(peer):
        return pl.ds(pl.multiple_of(peer * cols, cols), cols)

    def wo_part(head, group, core):
        at = head * cols + (group * 2 + core) * share
        return pl.ds(pl.multiple_of(at, share), share)

    own_rows = head_rows(my_head)
    copies = []

    def gather_rows(slot, peer):
        idx = src_ref[0, pl.ds(peer, 1), :]
        total = None
        rows = gx_ref.shape[1]
        step = 512
        for start in range(0, rows, step):
            at = lax.broadcasted_iota(jnp.int32, (step, cap), 0) + start
            pick = jnp.where(at == idx, 1.0, 0.0).astype(bf16)
            part = dot(gx_ref[:, start : start + step], pick)
            total = part if total is None else total + part
        rows_t[slot, padded - 16 : padded] = jnp.zeros((16, cap), bf16)
        rows_t[slot, :channels] = total.astype(bf16)

    gather_rows(n_grid, grid_peers[0])
    pl.semaphore_wait(barrier, n_grid - 1 + n_head - 1 + n_group - 1)
    edge_copies = [send_grid(0, 0, rows_t.at[n_grid], rows_t.at[my_grid])]
    mine_q = pl.ds(pl.multiple_of((my_group * 2 + core) * share, share), share)
    wo_head = [
        send(
            w_o_ref.at[mine_q],
            wo_full.at[wo_part(my_head, my_group, core)],
            ws_sem.at[d],
            wr_sem.at[d],
            {"head": head_peers[d]},
        )
        for d in range(n_head - 1)
    ]
    for d in range(1, n_grid - 1):
        gather_rows(n_grid + d, grid_peers[d])
        edge_copies.append(send_grid(0, d, rows_t.at[n_grid + d], rows_t.at[my_grid]))
    gather_rows(my_grid, my_grid)
    copies += edge_copies + wo_head
    wo_full[head_cols(my_head)] = w_o_ref[...]
    w_in_p[padded - 16 : padded] = jnp.zeros((16, width), bf16)
    w_in_p[:channels] = w_in_ref[...]
    same = lax.broadcasted_iota(jnp.int32, (n_grid, n_grid), 0) == lax.broadcasted_iota(
        jnp.int32, (n_grid, n_grid), 1
    )
    counts = jnp.sum(jnp.where(same, count_ref[...], 0).astype(f32), axis=1, keepdims=True)
    slot_at = lax.broadcasted_iota(jnp.int32, (n_grid, cap), 1).astype(f32)
    dst_live[...] = jnp.where(slot_at < counts, dst_ref[0], -1)

    mesh_f = mesh_ref[...].astype(f32)
    mesh_n = normalize(mesh_f)[0]
    x_t[:, n_grid * cap : n_grid * cap + nodes] = mesh_n.T.astype(bf16)
    mesh_n = mesh_n.astype(bf16)
    q_s[...] = dot(mesh_n, w_q_ref[...]).astype(bf16)
    kv_s[...] = dot(mesh_n, w_kv_ref[...]).astype(bf16)

    def onehots(s, carry):
        at = lax.broadcasted_iota(jnp.int32, (nodes, cap), 0)
        pick = jnp.where(at == dst_live[pl.ds(s, 1), :], 1.0, 0.0)
        hot_t[s] = pick.astype(bf16)
        hot[s] = pick.T.astype(bf16)
        return carry

    lax.fori_loop(0, n_grid, onehots, 0)

    row_at = lax.shift_right_logical(lax.broadcasted_iota(jnp.int32, (cols, cols), 0), 6)
    col_at = lax.shift_right_logical(lax.broadcasted_iota(jnp.int32, (cols, cols), 1), 6)
    same_head = jnp.where(row_at == col_at, 1.0, 0.0).astype(bf16)

    def head_sum(x):
        hi, lo = split(x)
        return dot(hi, same_head) + dot(lo, same_head)

    for c in edge_copies:
        c.wait_recv()

    def embed(s, carry):
        row = normalize(t_dot(rows_t[s], w_in_p[...]))[0]
        x_t[:, pl.ds(pl.multiple_of(s * cap, cap), cap)] = row.T.astype(bf16)
        kv[s] = dot(row.astype(bf16), w_kv_ref[...]).astype(bf16)
        return carry

    lax.fori_loop(0, n_grid, embed, 0)

    wo_group, wo_core = [], []
    for d in range(n_head - 1):
        wo_head[d].wait_recv()
        at = wo_part(head_from[d], my_group, core)
        for g in range(n_group - 1):
            to = {"groups": group_peers[g]}
            part = wo_full.at[at]
            wo_group.append(send(part, part, xs_sem.at[g, d], xr_sem.at[g, d], to))
        part = wo_full.at[at]
        wo_core.append(send(part, part, cs_sem.at[0, d], cr_sem.at[0, d], {"grid": sibling}))

    query = q_s[...]
    q_f = query.astype(f32)
    k_f = kv_s[:, :cols].astype(f32)
    v_f = kv_s[:, cols:].astype(f32)
    tanh_s = jnp.tanh(head_sum(q_f * k_f) * (scale / cap_limit))
    weight_s = jnp.exp(cap_limit * tanh_s)

    def scores(s, denom):
        q_e = dot(hot[s], query)
        t = jnp.tanh(head_sum(q_e * kv[s][:, :cols].astype(f32)) * (scale / cap_limit))
        w = jnp.exp(cap_limit * t)
        tanh_e[s] = t
        prob_e[s] = w
        return denom + dot_split(hot_t[s], w)

    denom = lax.fori_loop(0, n_grid, scores, weight_s)
    recip = 1.0 / denom
    prob_s = weight_s * recip
    recip_hi, recip_lo = split(recip)
    ps_b = prob_s.astype(bf16)

    def mix(s, total):
        p = prob_e[s] * (dot(hot[s], recip_hi) + dot(hot[s], recip_lo))
        prob_e[s] = p
        v = kv[s][:, cols:].astype(f32)
        return total + dot_split(hot_t[s], p.astype(bf16).astype(f32) * v)

    mixed = lax.fori_loop(0, n_grid, mix, ps_b.astype(f32) * v_f).astype(bf16)
    mixed_full[my_head] = mixed
    mix_copies = [
        send_head(0, d, mixed_full.at[my_head], mixed_full.at[my_head])
        for d in range(n_head - 1)
    ]

    node = lax.broadcasted_iota(jnp.int32, (nodes, nodes), 0)
    win = win_ref[...]
    count = jnp.zeros((nodes, nodes), f32)
    for m in range(win.shape[0]):
        count = count + jnp.where(node == win[m : m + 1, :], 1.0, 0.0)
    members[...] = count.T
    d_att = dot_t(cot_ref[...], w_po_ref[...]).astype(bf16)

    for g in range(n_group - 1):
        for d in range(n_head - 1):
            wo_group[d * (n_group - 1) + g].wait_recv()
            part = wo_full.at[wo_part(head_from[d], group_from[g], core)]
            to = {"grid": sibling}
            wo_core.append(send(part, part, cs_sem.at[g + 1, d], cr_sem.at[g + 1, d], to))
    copies += wo_group + wo_core + mix_copies

    def enc_term(head):
        return dot(mixed_full[head], wo_full[head_cols(head)]).astype(bf16).astype(f32)

    hm1 = mesh_f + enc_term(my_head)
    for c in wo_core:
        c.wait_recv()
    for d in range(n_head - 1):
        mix_copies[d].wait_recv()
        hm1 = hm1 + enc_term(head_from[d])
    hm1_s[...] = hm1
    normed = normalize(hm1)[0].astype(bf16)

    q2, k2, v2 = [dot(normed, w_pqkv_ref[t]).astype(bf16) for t in range(3)]
    col_head = lax.shift_right_logical(lax.broadcasted_iota(jnp.int32, (nodes, cols), 1), 6)
    zero = jnp.zeros((nodes, cols), f32)
    attended, d_q, d_k, d_v = zero, zero, zero, zero
    for h in range(heads):
        mine = col_head == h
        q_h = jnp.where(mine, q2.astype(f32), 0.0).astype(bf16)
        a_h = jnp.where(mine, d_att.astype(f32), 0.0).astype(bf16)
        tanh2 = jnp.tanh(dot_t(q_h, k2) * (scale / cap_limit))
        weight2 = members[...] * jnp.exp(cap_limit * tanh2)
        prob2 = weight2 / jnp.sum(weight2, axis=1, keepdims=True)
        pb = prob2.astype(bf16)
        attended = jnp.where(mine, dot(pb, v2), attended)
        dprob = dot_t(a_h, v2)
        ds = prob2 * (dprob - jnp.sum(prob2 * dprob, axis=1, keepdims=True))
        dz = ds * (1.0 - tanh2 * tanh2) * scale
        d_q = jnp.where(mine, dot(dz.astype(bf16), k2), d_q)
        d_k = jnp.where(mine, dot(dz.T.astype(bf16), q2), d_k)
        d_v = jnp.where(mine, dot(prob2.T.astype(bf16), d_att), d_v)
    back = dot_t(d_q.astype(bf16), w_pqkv_ref[0])
    back = back + dot_t(d_k.astype(bf16), w_pqkv_ref[1])
    back = back + dot_t(d_v.astype(bf16), w_pqkv_ref[2])
    back_send[...] = back.astype(bf16)
    back_copies = [
        send_head(1, d, back_send.at[head_rows(head_peers[d])], back_recv.at[d])
        for d in range(n_head - 1)
    ]
    copies += back_copies
    attended = attended.astype(bf16)
    for h in range(n_head):
        out_send[h] = dot(attended, w_po_ref[:, h * cols : (h + 1) * cols]).astype(bf16)
    xhat, inv = normalize(hm1_s[own_rows])
    for c in back_copies:
        c.wait_recv()
    d_n = back_send[own_rows].astype(f32)
    for d in range(n_head - 1):
        d_n = d_n + back_recv[d].astype(f32)
    d_n = d_n - jnp.mean(d_n, axis=1, keepdims=True) - xhat * jnp.mean(d_n * xhat, axis=1, keepdims=True)
    d_hm = (cot_ref[own_rows].astype(f32) + inv * d_n).astype(bf16)
    dm_rows = dot_t(d_hm, wo_full[...]).astype(bf16)
    for h in range(n_head):
        dm_send[h] = dm_rows[:, h * cols : (h + 1) * cols]
    dm_copies = [
        send_head(2, d, dm_send.at[head_peers[d]], dm_full.at[own_rows]) for d in range(n_head - 1)
    ]
    dm_full[own_rows] = dm_send[my_head]
    out_copies = [
        send_head(3, d, out_send.at[head_peers[d]], out_recv.at[d]) for d in range(n_head - 1)
    ]
    copies += dm_copies + out_copies
    for c in dm_copies:
        c.wait_recv()

    d_mixed = dm_full[...]
    dm_f = d_mixed.astype(f32)
    dprob_s = head_sum(dm_f * v_f)

    def inners(s, total):
        dprob = head_sum(dot(hot[s], d_mixed) * kv[s][:, cols:].astype(f32))
        return total + dot_split(hot_t[s], prob_e[s] * dprob)

    inner = lax.fori_loop(0, n_grid, inners, prob_s * dprob_s)
    in_hi, in_lo = split(inner)

    def edge_grads(s, carry):
        h = hot[s]
        q_e = dot(h, query)
        dm_e = dot(h, d_mixed)
        dprob = head_sum(dm_e * kv[s][:, cols:].astype(f32))
        t = tanh_e[s]
        p = prob_e[s]
        dz = p * (dprob - (dot(h, in_hi) + dot(h, in_lo))) * (1.0 - t * t) * scale
        at = pl.ds(pl.multiple_of(s * cap, cap), cap)
        grads[at, :cols] = (dz * q_e).astype(bf16)
        grads[at, cols:] = (p.astype(bf16).astype(f32) * dm_e).astype(bf16)
        return carry

    lax.fori_loop(0, n_grid, edge_grads, 0)
    dz_s = prob_s * (dprob_s - inner) * (1.0 - tanh_s * tanh_s) * scale
    grads[n_grid * cap : n_grid * cap + nodes, :cols] = (dz_s * q_f).astype(bf16)
    grads[n_grid * cap : n_grid * cap + nodes, cols:] = (ps_b.astype(f32) * dm_f).astype(bf16)

    def grad_term(pair, of_core):
        return dot(x_t[grid_rows(pair * 2 + of_core)], grads[...])

    pair_copies = []
    for j in range(n_pair):
        to_pair = pair_peers[j] if j < n_pair - 1 else my_pair
        pair_send[j] = grad_term(to_pair, 1 - core).astype(bf16)
        pair_copies.append(
            send(
                pair_send.at[j], pair_recv.at[j], ps_sem.at[j], pr_sem.at[j], {"grid": sibling}
            )
        )
    grad_copies = []
    for j in range(n_pair - 1):
        term = grad_term(pair_peers[j], core)
        pair_copies[j].wait_recv()
        grad_send[j] = (term + pair_recv[j].astype(f32)).astype(bf16)
        to = {"grid": pair_peers[j] * 2 + core}
        grad_copies.append(send(grad_send.at[j], grad_recv.at[j], gs_sem.at[1, j], gr_sem.at[1, j], to))
    copies += pair_copies + grad_copies
    grad_own = grad_term(my_pair, core)
    pair_copies[n_pair - 1].wait_recv()
    grad_own = grad_own + pair_recv[n_pair - 1].astype(f32)

    out_sum = out_send[my_head].astype(f32)
    for d in range(n_head - 1):
        out_copies[d].wait_recv()
        out_sum = out_sum + out_recv[d].astype(f32)
    hm_ref[...] = hm1_s[:, head_cols(my_head)] + out_sum

    for j in range(n_pair - 1):
        grad_copies[j].wait_recv()
        grad_own = grad_own + grad_recv[j].astype(f32)
    grad_ref[...] = grad_own
    for c in copies:
        c.wait_send()


def body(
    grid_x, mesh_h, w_in, w_q, w_kv, w_o, w_pqkv, w_po, edge_src, edge_dst, edge_count, win_idx, cot
):
    n_grid = lax.axis_size("grid")
    n_head = lax.axis_size("head")
    n_group = lax.axis_size("groups")
    cols = w_q.shape[1]
    nodes, width = mesh_h.shape
    cap = edge_src.shape[2]
    channels = grid_x.shape[1]
    own = nodes // n_head
    chunk = width // n_grid
    slots = n_grid * cap
    padded = channels + (-channels % 16)
    vmem = pl.BlockSpec(memory_space=pltpu.VMEM)
    hm, grad = pl.pallas_call(
        functools.partial(kernel, n_grid, n_head, n_group),
        out_shape=(
            jax.ShapeDtypeStruct((nodes, cols), f32),
            jax.ShapeDtypeStruct((chunk, 2 * cols), f32),
        ),
        in_specs=[vmem] * 13,
        out_specs=(vmem, vmem),
        scratch_shapes=[
            pltpu.VMEM((2 * n_grid - 1, padded, cap), bf16),
            pltpu.VMEM((width, slots + nodes), bf16),
            pltpu.VMEM((n_grid, cap, nodes), bf16),
            pltpu.VMEM((n_grid, nodes, cap), bf16),
            pltpu.VMEM((n_grid, cap, 2 * cols), bf16),
            pltpu.VMEM((n_grid, cap, cols), f32),
            pltpu.VMEM((n_grid, cap, cols), f32),
            pltpu.VMEM((slots + nodes, 2 * cols), bf16),
            pltpu.VMEM((nodes, cols), bf16),
            pltpu.VMEM((nodes, 2 * cols), bf16),
            pltpu.VMEM((nodes, nodes), f32),
            pltpu.VMEM((padded, width), bf16),
            pltpu.VMEM((n_grid, cap), jnp.int32),
            pltpu.VMEM((n_head * cols, width), bf16),
            pltpu.VMEM((n_head, nodes, cols), bf16),
            pltpu.VMEM((nodes, width), f32),
            pltpu.VMEM((n_head, nodes, cols), bf16),
            pltpu.VMEM((n_head - 1, nodes, cols), bf16),
            pltpu.VMEM((nodes, width), bf16),
            pltpu.VMEM((n_head - 1, own, width), bf16),
            pltpu.VMEM((n_head, own, cols), bf16),
            pltpu.VMEM((nodes, cols), bf16),
            pltpu.VMEM((n_grid // 2, chunk, 2 * cols), bf16),
            pltpu.VMEM((n_grid // 2, chunk, 2 * cols), bf16),
            pltpu.VMEM((n_grid // 2 - 1, chunk, 2 * cols), bf16),
            pltpu.VMEM((n_grid // 2 - 1, chunk, 2 * cols), bf16),
            pltpu.SemaphoreType.DMA((4, n_head - 1)),
            pltpu.SemaphoreType.DMA((4, n_head - 1)),
            pltpu.SemaphoreType.DMA((2, n_grid - 1)),
            pltpu.SemaphoreType.DMA((2, n_grid - 1)),
            pltpu.SemaphoreType.DMA((n_head - 1,)),
            pltpu.SemaphoreType.DMA((n_head - 1,)),
            pltpu.SemaphoreType.DMA((n_group - 1, n_head - 1)),
            pltpu.SemaphoreType.DMA((n_group - 1, n_head - 1)),
            pltpu.SemaphoreType.DMA((n_group, n_head - 1)),
            pltpu.SemaphoreType.DMA((n_group, n_head - 1)),
            pltpu.SemaphoreType.DMA((n_grid // 2,)),
            pltpu.SemaphoreType.DMA((n_grid // 2,)),
        ],
        compiler_params=pltpu.CompilerParams(
            collective_id=0, has_side_effects=True, vmem_limit_bytes=56 * 1024 * 1024
        ),
    )(
        grid_x.T,
        mesh_h,
        w_in,
        w_q,
        w_kv.reshape(width, 2 * cols),
        w_o,
        w_pqkv.transpose(1, 0, 2),
        w_po,
        edge_src,
        edge_dst,
        edge_count,
        win_idx.T,
        cot,
    )
    return hm.astype(bf16), grad.reshape(chunk, 2, cols)


def solution(mesh):
    placed = (
        P(("groups", "grid"), None),
        P(("groups", "grid"), None),
        P(),
        P(None, "head"),
        P(None, None, "head"),
        P("head", None),
        P(None, None, "head"),
        P("head", None),
        P("grid", None, None),
        P("grid", None, None),
        P("grid", None),
        P("grid", None),
        P(("groups", "grid"), None),
    )
    return jax.shard_map(
        body,
        mesh=mesh,
        in_specs=placed,
        out_specs=(P(("groups", "grid"), "head"), P(("groups", "grid"), None, "head")),
        check_vma=False,
    )
```

time: 108 us -> 84 us (0.78)
  the two profiles are of different devices: /device:TPU:29 before, /device:TPU:0 now
where the time goes in v2:
time: 84 us; the launch traced here: 83.6 us
  Pallas kernels  76.7 us (91%)
  local copies, waits for them, and re-layouts  4.6 us (5%)
  other arithmetic  1.62 us (2%)
    pallas_call x1, Pallas kernels, body(): pl.pallas_call(functools.partial(kernel, n_grid, n_head, n_group), out_sh...  76.7 us
    unnamed x1, local copies, waits for them, and re-layouts  2.44 us
    reshape x1, local copies, waits for them, and re-layouts, body(): return (hm.astype(bf16), grad.reshape(chunk, 2, cols))  2.16 us

profile of v2, /device:TPU:0, one launch (start us, length us, event | category | flops | bytes accessed | tf_op | source)
XLA Modules:
  0.0 83.6 jit_solution(16886157969146255370)
XLA Ops:
  0.6 2.4 %copy.15 = bf16[128,8,2,256]{3,1,2,0:T(8,128)(2,1)} copy(bf16[128,8,2,256]{3,2,1,0:T(2,128)(2,1)} %bitcast.7) | data formatting | bytes 2097152
  3.1 76.7 %shard_map.140 = (f32[256,256]{1,0:T(8,128)}, f32[256,512]{1,0:T(8,128)}) custom-call(bf16[100,2048]{1,0:T(8,128)(2,1)} %bitcast.8, bf16[256,1024]{1,0:T(8,128)(2,1)} %mesh_ref.1, bf16[100,1024]{1,0:T(8,128)(2,1)} %w_in_ref.1, bf16[1024,256]{1,0:T(8,128)(2,1)} %w_q_ref.1, bf16[1024,512]{1,0:T(8,128)(2,1)} %bitcast.5, bf16[256,1024]{1,0:T(8,128)(2,1)} %w_o_ref.1, ...), custom_call_target="tpu_custom_call" | custom-call | tf_op jit(solution)/shard_map/pallas_call | solution.py:465
  79.8 1.6 %convert_element_type.3 = bf16[256,256]{1,0:T(8,128)(2,1)} convert(f32[256,256]{1,0:T(8,128)} %get-tuple-element.4) | non-fusion elementwise | flops 65536 | bytes 393216 | tf_op jit(solution)/shard_map/convert_element_type | solution.py:531
  81.4 2.2 %reshape.11 = f32[256,2,256]{2,1,0:T(2,128)} reshape(f32[256,512]{1,0:T(8,128)} %get-tuple-element.5) | data formatting | bytes 1048576 | tf_op jit(solution)/shard_map/reshape | solution.py:531

commit v3 on v2

--- a/solution.py
+++ b/solution.py
@@ -79,6 +79,7 @@
     q_s,
     kv_s,
     members,
+    w_kv2,
     w_in_p,
     dst_live,
     wo_full,
@@ -212,6 +213,8 @@
     wo_full[head_cols(my_head)] = w_o_ref[...]
     w_in_p[padded - 16 : padded] = jnp.zeros((16, width), bf16)
     w_in_p[:channels] = w_in_ref[...]
+    for t in range(2):
+        w_kv2[:, t * cols : (t + 1) * cols] = w_kv_ref[:, t, :]
     same = lax.broadcasted_iota(jnp.int32, (n_grid, n_grid), 0) == lax.broadcasted_iota(
         jnp.int32, (n_grid, n_grid), 1
     )
@@ -224,7 +227,7 @@
     x_t[:, n_grid * cap : n_grid * cap + nodes] = mesh_n.T.astype(bf16)
     mesh_n = mesh_n.astype(bf16)
     q_s[...] = dot(mesh_n, w_q_ref[...]).astype(bf16)
-    kv_s[...] = dot(mesh_n, w_kv_ref[...]).astype(bf16)
+    kv_s[...] = dot(mesh_n, w_kv2[...]).astype(bf16)
 
     def onehots(s, carry):
         at = lax.broadcasted_iota(jnp.int32, (nodes, cap), 0)
@@ -249,11 +252,27 @@
     def embed(s, carry):
         row = normalize(t_dot(rows_t[s], w_in_p[...]))[0]
         x_t[:, pl.ds(pl.multiple_of(s * cap, cap), cap)] = row.T.astype(bf16)
-        kv[s] = dot(row.astype(bf16), w_kv_ref[...]).astype(bf16)
+        kv[s] = dot(row.astype(bf16), w_kv2[...]).astype(bf16)
         return carry
 
     lax.fori_loop(0, n_grid, embed, 0)
 
+    query = q_s[...]
+    q_f = query.astype(f32)
+    k_f = kv_s[:, :cols].astype(f32)
+    v_f = kv_s[:, cols:].astype(f32)
+    tanh_s = jnp.tanh(head_sum(q_f * k_f) * (scale / cap_limit))
+    weight_s = jnp.exp(cap_limit * tanh_s)
+
+    def scores(s, denom):
+        q_e = dot(hot[s], query)
+        t = jnp.tanh(head_sum(q_e * kv[s][:, :cols].astype(f32)) * (scale / cap_limit))
+        w = jnp.exp(cap_limit * t)
+        tanh_e[s] = t
+        prob_e[s] = w
+        return denom + dot_split(hot_t[s], w)
+
+    denom = lax.fori_loop(0, n_grid, scores, weight_s)
     wo_group, wo_core = [], []
     for d in range(n_head - 1):
         wo_head[d].wait_recv()
@@ -265,22 +284,6 @@
         part = wo_full.at[at]
         wo_core.append(send(part, part, cs_sem.at[0, d], cr_sem.at[0, d], {"grid": sibling}))
 
-    query = q_s[...]
-    q_f = query.astype(f32)
-    k_f = kv_s[:, :cols].astype(f32)
-    v_f = kv_s[:, cols:].astype(f32)
-    tanh_s = jnp.tanh(head_sum(q_f * k_f) * (scale / cap_limit))
-    weight_s = jnp.exp(cap_limit * tanh_s)
-
-    def scores(s, denom):
-        q_e = dot(hot[s], query)
-        t = jnp.tanh(head_sum(q_e * kv[s][:, :cols].astype(f32)) * (scale / cap_limit))
-        w = jnp.exp(cap_limit * t)
-        tanh_e[s] = t
-        prob_e[s] = w
-        return denom + dot_split(hot_t[s], w)
-
-    denom = lax.fori_loop(0, n_grid, scores, weight_s)
     recip = 1.0 / denom
     prob_s = weight_s * recip
     recip_hi, recip_lo = split(recip)
@@ -373,12 +376,12 @@
         send_head(2, d, dm_send.at[head_peers[d]], dm_full.at[own_rows]) for d in range(n_head - 1)
     ]
     dm_full[own_rows] = dm_send[my_head]
+    for c in dm_copies:
+        c.wait_recv()
     out_copies = [
         send_head(3, d, out_send.at[head_peers[d]], out_recv.at[d]) for d in range(n_head - 1)
     ]
     copies += dm_copies + out_copies
-    for c in dm_copies:
-        c.wait_recv()
 
     d_mixed = dm_full[...]
     dm_f = d_mixed.astype(f32)
@@ -482,6 +485,7 @@
             pltpu.VMEM((nodes, cols), bf16),
             pltpu.VMEM((nodes, 2 * cols), bf16),
             pltpu.VMEM((nodes, nodes), f32),
+            pltpu.VMEM((width, 2 * cols), bf16),
             pltpu.VMEM((padded, width), bf16),
             pltpu.VMEM((n_grid, cap), jnp.int32),
             pltpu.VMEM((n_head * cols, width), bf16),
@@ -518,7 +522,7 @@
         mesh_h,
         w_in,
         w_q,
-        w_kv.reshape(width, 2 * cols),
+        w_kv,
         w_o,
         w_pqkv.transpose(1, 0, 2),
         w_po,

time: 84 us -> 77.9 us (0.927)
  Pallas kernels: 76.7 us -> 73.3 us
  local copies, waits for them, and re-layouts: 4.6 us -> 2.16 us
    pallas_call x1, Pallas kernels: 76.7 us -> 73.3 us  [body(): pl.pallas_call(functools.partial(kernel, n_grid, n_head, n_group), out_sh...]
    unnamed x1 -> x0, local copies, waits for them, and re-layouts: 2.44 us -> none
where the time goes in v3:
time: 77.9 us; the launch traced here: 77.7 us
  Pallas kernels  73.3 us (94%)
  local copies, waits for them, and re-layouts  2.16 us (3%)
  other arithmetic  1.62 us (2%)
    pallas_call x1, Pallas kernels, body(): pl.pallas_call(functools.partial(kernel, n_grid, n_head, n_group), out_sh...  73.3 us
    reshape x1, local copies, waits for them, and re-layouts, body(): return (hm.astype(bf16), grad.reshape(chunk, 2, cols))  2.16 us
    convert_element_type x1, other arithmetic, body(): return (hm.astype(bf16), grad.reshape(chunk, 2, cols))  1.62 us

profile of v3, /device:TPU:0, one launch (start us, length us, event | category | flops | bytes accessed | tf_op | source)
XLA Modules:
  0.0 77.7 jit_solution(770708535907389546)
XLA Ops:
  0.6 73.3 %shard_map.140 = (f32[256,256]{1,0:T(8,128)}, f32[256,512]{1,0:T(8,128)}) custom-call(bf16[100,2048]{1,0:T(8,128)(2,1)} %bitcast.4, bf16[256,1024]{1,0:T(8,128)(2,1)} %mesh_ref.1, bf16[100,1024]{1,0:T(8,128)(2,1)} %w_in_ref.1, bf16[1024,256]{1,0:T(8,128)(2,1)} %w_q_ref.1, bf16[1024,2,256]{2,1,0:T(2,128)(2,1)} %w_kv_ref.1, bf16[256,1024]{1,0:T(8,128)(2,1)} %w_o_ref.1, ...), custom_call_target="tpu_custom_call" | custom-call | tf_op jit(solution)/shard_map/pallas_call | solution.py:468
  73.9 1.6 %convert_element_type.3 = bf16[256,256]{1,0:T(8,128)(2,1)} convert(f32[256,256]{1,0:T(8,128)} %get-tuple-element.4) | non-fusion elementwise | flops 65536 | bytes 393216 | tf_op jit(solution)/shard_map/convert_element_type | solution.py:535
  75.6 2.2 %reshape.7 = f32[256,2,256]{2,1,0:T(2,128)} reshape(f32[256,512]{1,0:T(8,128)} %get-tuple-element.5) | data formatting | bytes 1048576 | tf_op jit(solution)/shard_map/reshape | solution.py:535
